TPU v7x, 512 devices: a whole 4x4x16 slice. The times are simulated.
512 devices in a mesh: dp: 32 (over x_hi, z), mp: 16 (over y, x_lo, core).
Axes of the slice: x: 4 (x_hi: 2, x_lo: 2; x = x_hi * 2 + x_lo), y: 4, z: 16, core: 2. Of those that a mesh axis runs over, the one named last changes fastest.
Arguments:
- grad_out: bfloat16 [16384, 6144], P('dp', 'mp'), may hold values from -200 to 200
- queries: bfloat16 [16384, 4096], P('dp', 'mp'), may hold values from -6.5 to 6.5
- key_rows: bfloat16 [16384, 4096], P('dp', 'mp'), may hold values from -6.5 to 6.5
- value_rows: bfloat16 [16384, 4096], P('dp', 'mp'), may hold values from -200 to 200
- out_weight: bfloat16 [4096, 6144], P('mp', 'dp'), may hold values from -0.09375 to 0.09375
- scale_exponent: int32 [], replicated, may hold values from 4 to 12
Outputs:
- grad_query: bfloat16 [16384, 4096], P('dp', 'mp')
- grad_key: bfloat16 [16384, 4096], P('dp', 'mp')
- grad_value: bfloat16 [16384, 4096], P('dp', 'mp')
- grad_weight: bfloat16 [4096, 6144], P('mp', 'dp')
- headroom: float32 [], replicated
- grad_magnitude: float32 [], replicated
All inputs are finite; a program needn't handle non-finite values. Where the computation divides by a largest or mean magnitude, that divisor is 1e-20 or more.
Results may differ from a plain program's by a relative error of at most 0.025.
Values may be sent and summed in bfloat16 or wider, within the bound.
A program may use at most 64 MiB of HBM per device.

v0:
```python
import jax
import jax.numpy as jnp
from jax import lax
from jax.sharding import PartitionSpec as P

D = 6144
H = 32
HD = 128
SEQ = 256


OVERFLOW_BOUND = 65504.0
EPSILON = 1e-06


def split_heads(matrix):
    tokens, columns = matrix.shape
    return matrix.reshape(tokens // SEQ, SEQ, columns // HD, HD)


def join_heads(tensor):
    images, length, head_count, depth = tensor.shape
    return tensor.reshape(images * length, head_count * depth)


def attention_forward(queries, key_rows, value_rows):
    factor = HD ** (-0.5)
    scores = (
        jnp.einsum(
            "bqhd,bkhd->bhqk",
            split_heads(queries),
            split_heads(key_rows),
            preferred_element_type=jnp.float32,
        )
        * factor
    )
    maxima = jnp.max(scores, axis=-1, keepdims=True)
    raised = jnp.exp(scores - maxima)
    attention = raised / jnp.sum(raised, axis=-1, keepdims=True)
    attention_low = attention.astype(jnp.bfloat16)
    context = jnp.einsum(
        "bhqk,bkhd->bqhd",
        attention_low,
        split_heads(value_rows),
        preferred_element_type=jnp.float32,
    )
    return (attention, attention_low, join_heads(context.astype(jnp.bfloat16)))


def attention_backward(
    queries, key_rows, value_rows, attention, attention_low, grad_context, inverse
):
    factor = HD ** (-0.5)
    query_split = split_heads(queries)
    key_split = split_heads(key_rows)
    grad_split = split_heads(grad_context)
    grad_value = jnp.einsum(
        "bhqk,bqhd->bkhd", attention_low, grad_split, preferred_element_type=jnp.float32
    )
    grad_attention = jnp.einsum(
        "bqhd,bkhd->bhqk", grad_split, split_heads(value_rows), preferred_element_type=jnp.float32
    )
    row_dots = jnp.sum(attention * grad_attention, axis=-1, keepdims=True)
    grad_scores = (attention * (grad_attention - row_dots) * factor).astype(jnp.bfloat16)
    grad_query = jnp.einsum(
        "bhqk,bkhd->bqhd", grad_scores, key_split, preferred_element_type=jnp.float32
    )
    grad_key = jnp.einsum(
        "bhqk,bqhd->bkhd", grad_scores, query_split, preferred_element_type=jnp.float32
    )

    def finish(tensor):
        return join_heads((tensor * inverse).astype(jnp.bfloat16))

    return (finish(grad_query), finish(grad_key), finish(grad_value))


def shards(grad_out, queries, key_rows, value_rows, out_weight, scale_exponent):
    exponent = scale_exponent.astype(jnp.float32)
    scaling = jnp.exp2(exponent)
    inverse = jnp.exp2(-exponent)
    grad_scaled = (grad_out.astype(jnp.float32) * scaling).astype(jnp.bfloat16)
    weight_full = lax.all_gather(out_weight, "dp", axis=1, tiled=True)
    attention, attention_low, context = attention_forward(queries, key_rows, value_rows)
    grad_full = lax.all_gather(grad_scaled, "mp", axis=1, tiled=True)
    grad_context = jnp.einsum(
        "td,hd->th", grad_full, weight_full, preferred_element_type=jnp.float32
    ).astype(jnp.bfloat16)
    partial_value = jnp.einsum(
        "th,td->hd", context, grad_full, preferred_element_type=jnp.float32
    ).astype(jnp.bfloat16)
    summed = lax.psum_scatter(
        partial_value.astype(jnp.float32).astype(jnp.bfloat16),
        "dp",
        scatter_dimension=1,
        tiled=True,
    ).astype(jnp.float32)
    grad_query, grad_key, grad_value = attention_backward(
        queries, key_rows, value_rows, attention, attention_low, grad_context, inverse
    )
    unscaled = summed * inverse
    local_squares = jnp.sum(unscaled * unscaled)
    local_largest = jnp.max(jnp.abs(summed))
    square_total = lax.psum(local_squares, ("dp", "mp"))
    largest = lax.pmax(local_largest, ("dp", "mp"))
    grad_magnitude = jnp.sqrt(square_total / float(H * HD * D) + EPSILON)
    clipping = jnp.minimum(1.0, 1.0 / grad_magnitude)
    grad_weight = (unscaled * clipping).astype(jnp.bfloat16)
    headroom = jnp.log2(OVERFLOW_BOUND / (largest + EPSILON))
    return (grad_query, grad_key, grad_value, grad_weight, headroom, grad_magnitude)


def solution(mesh):
    placed = (P("dp", "mp"), P("dp", "mp"), P("dp", "mp"), P("dp", "mp"), P("mp", "dp"), P())
    return jax.shard_map(
        shards,
        mesh=mesh,
        in_specs=placed,
        out_specs=(P("dp", "mp"), P("dp", "mp"), P("dp", "mp"), P("mp", "dp"), P(), P()),
        check_vma=False,
    )
```

profile of v0, /device:TPU:1, one launch (start us, length us, event | category | flops | bytes accessed | tf_op | source)
XLA Modules:
  0.0 1116.1 jit_solution(12029370245412100648)
XLA Ops:
  7.2 0.0 all-gather.3.cloned.1.call-start
  7.9 1.8 multiply_convert_fusion
  9.7 0.0 all-gather.3.cloned.1.call-update
  9.7 0.0 all-gather.5.cloned.1.call-start
  9.8 0.7 all-gather.5.cloned.1.call-update
  10.5 0.0 reduce-scatter.2.cloned.1.call-start
  10.5 1.0 reshape.45
  11.6 1.0 reshape.43
  12.6 1.0 reshape.42
  13.6 0.5 fusion.67
  14.1 0.8 fusion.11
  14.9 0.3 copy.37
  15.2 51.0 %all-gather.3.cloned.1.call-done = bf16[512,6144]{1,0:T(8,128)(2,1)} async-done(((bf16[512,384]{1,0:T(8,128)(2,1)}), bf16[512,6144]{1,0:T(8,128)(2,1)}) %all-gather.3.cloned.1.call-update) | async-done | bytes 6291472 | tf_op jit(solution)/shard_map/all_gather | solution.py:85
  66.2 7.0 convolution_convert_fusion
  73.2 0.0 reduce-scatter.2.cloned.1.call-update
  73.2 144.1 %all-gather.5.cloned.1.call-done = bf16[256,6144]{0,1:T(8,128)(2,1)} async-done(((bf16[256,192]{0,1:T(8,128)(2,1)}), bf16[256,6144]{0,1:T(8,128)(2,1)}) %all-gather.5.cloned.1.call-update) | async-done | bytes 3145744 | tf_op jit(solution)/shard_map/all_gather | solution.py:83
  217.4 5.5 convolution_convert_fusion.1
  222.9 0.1 reshape.44
  222.9 0.1 copy.32
  223.1 0.3 fusion.28
  223.4 0.6 fusion.14
  224.0 0.3 copy.29
  224.2 0.7 copy.92
  225.0 0.7 fusion.12
  225.7 0.2 copy.34
  225.9 0.5 fusion.13
  226.3 0.3 copy.31
  226.6 0.9 copy_bitcast_fusion
  227.5 663.3 %reduce-scatter.2.cloned.1.call-done = bf16[256,192]{0,1:T(8,128)(2,1)} async-done(((bf16[256,6144]{0,1:T(8,128)(2,1)}), bf16[256,192]{0,1:T(8,128)(2,1)}) %reduce-scatter.2.cloned.1.call-update) | async-done | bytes 98320 | tf_op jit(solution)/shard_map/reduce_scatter | solution.py:92
  890.8 1.5 fusion.36
  892.4 112.2 %psum.7 = f32[]{:T(128)} all-reduce(f32[]{:T(128)} %get-tuple-element.7), channel_id=1, replica_groups=mesh['dp'=32,'mp'=16] {'dp','mp'}, use_global_device_ids=true, to_apply=%region_5.0 | all-reduce | flops 1 | bytes 8 | tf_op jit(solution)/shard_map/psum | solution.py:104
  1005.3 99.7 %pmax.7 = f32[]{:T(128)} all-reduce(f32[]{:T(128)} %get-tuple-element.6), channel_id=1, replica_groups=mesh['dp'=32,'mp'=16] {'dp','mp'}, use_global_device_ids=true, to_apply=%region_7.0 | all-reduce | flops 1 | bytes 8 | tf_op jit(solution)/shard_map/pmax | solution.py:105
  1105.8 1.6 fusion.35
Async XLA Ops:
  7.2 59.0 %all-gather.3.cloned.1.call-start = ((), (), s32[]{:S(2)}) async-start(), calls=%async_computation.1 | async-start | bytes 6684672 | tf_op jit(solution)/shard_map/all_gather | solution.py:85
  9.7 207.6 %all-gather.5.cloned.1.call-start = ((), (), s32[]{:S(2)}) async-start(), calls=%async_computation.2 | async-start | bytes 3244032 | tf_op jit(solution)/shard_map/all_gather | solution.py:83
  10.5 880.3 %reduce-scatter.2.cloned.1.call-start = ((), (), s32[]{:S(2)}) async-start(), calls=%async_computation.3 | async-start | bytes 3244032 | tf_op jit(solution)/shard_map/reduce_scatter | solution.py:92
Sparse Core Ops, SparseCore 0:
  10.1 56.0 all-gather.2
  69.3 148.0 all-gather.4
  221.8 668.9 reduce-scatter.1
where the time goes:
time: 1120 us
  waiting for transfers between devices  859 us (77%)
  blocking collectives  212 us (19%)
  between operations  18.3 us (2%)
  matrix products  15.8 us (1%)
    reduce_scatter x1, waiting for transfers between devices, shards(): lax.psum_scatter(partial_value.astype(jnp.float32).astype(jnp.bfloat16),...  663 us
    all_gather x1, waiting for transfers between devices, shards(): weight_full = lax.all_gather(out_weight, 'dp', axis=1, tiled=True)  144 us
    psum x1, blocking collectives, shards(): square_total = lax.psum(local_squares, ('dp', 'mp'))  112 us
    pmax x1, blocking collectives, shards(): largest = lax.pmax(local_largest, ('dp', 'mp'))  99.7 us
    all_gather x1, waiting for transfers between devices, shards(): grad_full = lax.all_gather(grad_scaled, 'mp', axis=1, tiled=True)  51 us
  transfers between devices with their start and end apart: 3, of which 3 were waited for; matrix products, arithmetic and copies ran while one was open for 2% of the time, Pallas kernels for 0%

commit v1 on v0

v1 whole, which is shorter than its diff:
```python
import jax
import jax.numpy as jnp
from jax import lax
from jax.experimental import pallas as pl
from jax.experimental.pallas import tpu as pltpu
from jax.sharding import PartitionSpec as P

D = 6144
H = 32
HD = 128
SEQ = 256
NZ = 16
NY = 4
TOK = 512
MINE = 384
HEADS = 256
COLS = 192

OVERFLOW_BOUND = 65504.0
EPSILON = 1e-06
MESH = pl.DeviceIdType.MESH
F32 = jnp.float32
BF16 = jnp.bfloat16


def dot(a, b, contract=((1,), (0,))):
    return lax.dot_general(a, b, (contract, ((), ())), preferred_element_type=F32)


def kernel(
    exponent_ref, grad_ref, q_ref, k_ref, v_ref, w_ref,
    gq_ref, gk_ref, gv_ref, gw_ref, headroom_ref, magnitude_ref,
    gf, wt, part, hop, xout, xin, att, ctx_t, acc, gc, own_sum, dp_stats, mp_stats,
    g_send, g_recv, sib_send, sib_recv, w_send, w_recv, wx_send, wx_recv,
    r_send, r_recv, x_send, x_recv, s_send, s_recv, t_send, t_recv,
):
    dp = lax.axis_index("dp")
    mp = lax.axis_index("mp")
    xh, z = dp // NZ, dp % NZ
    y, xl, c = mp // 4, (mp // 2) % 2, mp % 2
    factor = HD ** (-0.5)

    def chip(yy, xx):
        return ((yy + NY) % NY) * 2 + xx

    def to_mp(index):
        return {"dp": dp, "mp": index}

    def to_dp(index):
        return {"dp": index, "mp": mp}

    up, down = to_mp(chip(y + 1, xl) * 2 + c), to_mp(chip(y - 1, xl) * 2 + c)
    across = to_mp(chip(y, 1 - xl) * 2 + c)
    sibling = to_mp(chip(y, xl) * 2 + 1 - c)
    right, left = to_dp(xh * NZ + (z + 1) % NZ), to_dp(xh * NZ + (z + NZ - 1) % NZ)
    far = to_dp((1 - xh) * NZ + z)

    barrier = pltpu.get_barrier_semaphore()

    def greet_dp(i, _):
        pl.semaphore_signal(barrier, inc=1, device_id=to_dp((dp + i) % 32), device_id_type=MESH)
        return 0

    def greet_mp(i, _):
        pl.semaphore_signal(barrier, inc=1, device_id=to_mp((mp + i) % 16), device_id_type=MESH)
        return 0

    lax.fori_loop(1, 32, greet_dp, 0)
    lax.fori_loop(1, 16, greet_mp, 0)

    exponent = exponent_ref[0]
    scaling = lax.shift_left(jnp.int32(1), exponent).astype(F32)
    inverse = lax.shift_left(jnp.int32(1), 24 - exponent).astype(F32) * (2.0 ** -24)

    for h in range(2):
        gf[mp, h] = (grad_ref[h * SEQ : (h + 1) * SEQ, :].astype(F32) * scaling).astype(BF16)
    wt[xh, z] = w_ref[...].astype(F32).T.astype(BF16)

    pl.semaphore_wait(barrier, 46)

    def g_copy(p, h, slot, target):
        piece = gf.at[p * 2 + c, h]
        return pltpu.make_async_remote_copy(
            piece, piece, g_send.at[slot], g_recv.at[p, h], device_id=target, device_id_type=MESH
        )

    def g_wait(p, h):
        g_copy(p, h, 0, across).wait_recv()

    def sib_copy(p, cc):
        piece = gf.at[p * 2 + cc]
        return pltpu.make_async_remote_copy(
            piece, piece, sib_send.at[p], sib_recv.at[p], device_id=sibling, device_id_type=MESH
        )

    me = chip(y, xl)
    peer = chip(y, 1 - xl)
    above, below, opposite = chip(y + 1, xl), chip(y - 1, xl), chip(y + 2, xl)
    above_peer, below_peer, opposite_peer = (
        chip(y + 1, 1 - xl), chip(y - 1, 1 - xl), chip(y + 2, 1 - xl))

    def w_copy(step, direction):
        index = (z + NZ - step) % NZ if direction == 0 else (z + step) % NZ
        piece = wt.at[xh, index]
        return pltpu.make_async_remote_copy(
            piece, piece, w_send.at[direction, step], w_recv.at[direction, step],
            device_id=right if direction == 0 else left, device_id_type=MESH,
        )

    def w_arrived(step, direction):
        index = (z + NZ - step - 1) % NZ if direction == 0 else (z + step + 1) % NZ
        piece = wt.at[xh, index]
        pltpu.make_async_remote_copy(
            piece, piece, w_send.at[direction, step], w_recv.at[direction, step],
            device_id=right if direction == 0 else left, device_id_type=MESH,
        ).wait_recv()

    def w_step(step):
        for direction in range(2):
            w_arrived(step - 1, direction)
            if step < (8, 7)[direction]:
                w_copy(step, direction).start()

    def wx_copy(index, half):
        piece = wt.at[half, index]
        return pltpu.make_async_remote_copy(
            piece, piece, wx_send.at[index], wx_recv.at[index], device_id=far, device_id_type=MESH
        )

    def partial_of(m):
        block = dot(ctx_t[...], gf[m].reshape(TOK, MINE))
        turned = block.T.astype(BF16)
        part[m // 8, 2 * (m % 8)] = turned[:COLS]
        part[m // 8, 2 * (m % 8) + 1] = turned[COLS:]

    def sib_partial(p):
        sib_copy(p, 1 - c).wait_recv()
        partial_of(p * 2 + 1 - c)

    g_copy(me, 0, 0, across).start()
    g_copy(me, 0, 1, up).start()
    g_copy(me, 1, 2, down).start()
    w_copy(0, 0).start()
    w_copy(0, 1).start()
    g_copy(me, 1, 3, across).start()
    g_copy(me, 1, 4, up).start()
    g_copy(me, 0, 5, down).start()
    sib_copy(me, c).start()

    for b in range(2):
        for h in range(2):
            rows, lanes = slice(b * SEQ, (b + 1) * SEQ), slice(h * HD, (h + 1) * HD)
            scores = dot(q_ref[rows, lanes], k_ref[rows, lanes], ((1,), (1,))) * factor
            raised = jnp.exp(scores - jnp.max(scores, axis=-1, keepdims=True))
            attention = raised / jnp.sum(raised, axis=-1, keepdims=True)
            att[b * 2 + h] = attention
            context = dot(attention.astype(BF16), v_ref[rows, lanes])
            ctx_t[lanes, rows] = context.T.astype(BF16)

    w_step(1)
    g_wait(below, 0)
    g_copy(below, 0, 6, up).start()
    g_wait(above, 1)
    g_copy(above, 1, 7, down).start()
    w_step(2)
    partial_of(mp)
    g_wait(peer, 0)
    g_copy(peer, 0, 8, up).start()
    g_copy(peer, 0, 9, down).start()
    g_wait(peer, 1)
    g_copy(peer, 1, 10, up).start()
    g_copy(peer, 1, 11, down).start()
    sib_copy(peer, c).start()
    g_wait(below, 1)
    sib_copy(below, c).start()
    g_wait(above, 0)
    sib_copy(above, c).start()
    w_step(3)
    sib_partial(me)
    partial_of(peer * 2 + c)
    partial_of(below * 2 + c)
    partial_of(above * 2 + c)
    w_step(4)
    g_wait(opposite, 0)
    g_copy(opposite, 0, 12, across).start()
    g_wait(opposite, 1)
    g_copy(opposite, 1, 13, across).start()
    sib_copy(opposite, c).start()
    partial_of(opposite * 2 + c)
    w_step(5)
    sib_partial(peer)
    sib_partial(below)
    sib_partial(above)
    sib_partial(opposite)
    w_step(6)
    for p in (below_peer, above_peer, opposite_peer):
        g_wait(p, 0)
        g_wait(p, 1)
        sib_copy(p, c).start()
    for p in (below_peer, above_peer, opposite_peer):
        partial_of(p * 2 + c)
    w_step(7)
    for p in (below_peer, above_peer, opposite_peer):
        sib_partial(p)

    def r_copy(step, direction, half, source):
        return pltpu.make_async_remote_copy(
            source, hop.at[direction, step, half],
            r_send.at[direction, step, half], r_recv.at[direction, step, half],
            device_id=right if direction == 0 else left, device_id_type=MESH,
        )

    def r_dest(step, direction):
        return (z + 8 - step) % NZ if direction == 0 else (z + NZ - 7 + step) % NZ

    def r_arrived(step, direction, half):
        r_copy(step, direction, half, hop.at[direction, step, half]).wait_recv()

    def r_forward(step, direction, half):
        slot = hop.at[direction, step - 1, half]
        r_arrived(step - 1, direction, half)
        slot[...] = (
            slot[...].astype(F32) + part[half, r_dest(step, direction)].astype(F32)
        ).astype(BF16)
        r_copy(step, direction, half, slot).start()

    for half in range(2):
        for direction in range(2):
            r_copy(0, direction, half, part.at[half, r_dest(0, direction)]).start()

    w_arrived(7, 0)

    def wx_start(i, _):
        wx_copy((z + i) % NZ, xh).start()
        return 0

    lax.fori_loop(0, NZ, wx_start, 0)

    def r_step(step, _):
        for half in range(2):
            for direction in range(2):
                r_forward(step, direction, half)
        return 0

    lax.fori_loop(1, 7, r_step, 0)
    for half in range(2):
        r_forward(7, 0, half)
    for half in range(2):
        r_arrived(6, 1, half)
    for half in range(2):
        r_arrived(7, 0, half)

    def total(half):
        return (
            part[half, z].astype(F32) + hop[0, 7, half].astype(F32) + hop[1, 6, half].astype(F32)
        )

    xout[...] = total(1 - xh).astype(BF16)
    crossing = pltpu.make_async_remote_copy(
        xout, xin, x_send, x_recv, device_id=far, device_id_type=MESH
    )
    crossing.start()
    own_sum[...] = total(xh)
    crossing.wait_recv()
    summed = own_sum[...] + xin[...].astype(F32)
    own_sum[...] = summed

    unscaled = summed * inverse
    squared = unscaled * unscaled
    dp_stats[0, 0] = jnp.sum(
        (squared[:, :128] + squared[:, 128:]).reshape(COLS // 8, 8, 128), axis=0
    )
    size = jnp.abs(summed)
    dp_stats[0, 1] = jnp.max(
        jnp.maximum(size[:, :128], size[:, 128:]).reshape(COLS // 8, 8, 128), axis=0
    )

    def s_copy(i):
        return pltpu.make_async_remote_copy(
            dp_stats.at[0], dp_stats.at[i], s_send.at[i], s_recv.at[i],
            device_id=to_dp((dp + i) % 32), device_id_type=MESH,
        )

    def t_copy(i):
        return pltpu.make_async_remote_copy(
            mp_stats.at[0], mp_stats.at[i], t_send.at[i], t_recv.at[i],
            device_id=to_mp((mp + i) % 16), device_id_type=MESH,
        )

    def start(copy):
        def body(i, _):
            copy(i).start()
            return 0
        return body

    def arrive(copy):
        def body(i, _):
            copy(i).wait_recv()
            return 0
        return body

    def leave(copy):
        def body(i, _):
            copy(i).wait_send()
            return 0
        return body

    lax.fori_loop(1, 32, start(s_copy), 0)

    def wx_arrive(i, _):
        wx_copy((z + i) % NZ, 1 - xh).wait_recv()
        return 0

    lax.fori_loop(0, NZ, wx_arrive, 0)
    acc[...] = jnp.zeros_like(acc)

    def add_context(m, _):
        rows = wt[m // 8, pl.ds(2 * (m % 8), 2)].reshape(MINE, HEADS)
        acc[...] += dot(gf[m].reshape(TOK, MINE), rows)
        return 0

    lax.fori_loop(0, 16, add_context, 0)
    gc[...] = acc[...].astype(BF16)

    lax.fori_loop(1, 32, arrive(s_copy), 0)
    mp_stats[0, 0] = jnp.sum(dp_stats[:, 0], axis=0)
    mp_stats[0, 1] = jnp.max(dp_stats[:, 1], axis=0)
    lax.fori_loop(1, 16, start(t_copy), 0)

    for b in range(2):
        for h in range(2):
            rows, lanes = slice(b * SEQ, (b + 1) * SEQ), slice(h * HD, (h + 1) * HD)
            attention = att[b * 2 + h]
            grad = gc[rows, lanes]
            gv_ref[rows, lanes] = (dot(attention.T.astype(BF16), grad) * inverse).astype(BF16)
            grad_attention = dot(grad, v_ref[rows, lanes], ((1,), (1,)))
            row_dots = jnp.sum(attention * grad_attention, axis=-1, keepdims=True)
            grad_scores = attention * (grad_attention - row_dots) * factor
            gq_ref[rows, lanes] = (
                dot(grad_scores.astype(BF16), k_ref[rows, lanes]) * inverse
            ).astype(BF16)
            gk_ref[rows, lanes] = (
                dot(grad_scores.T.astype(BF16), q_ref[rows, lanes]) * inverse
            ).astype(BF16)

    lax.fori_loop(1, 16, arrive(t_copy), 0)
    squares = jnp.sum(jnp.sum(mp_stats[:, 0], axis=0), keepdims=True)
    largest = jnp.max(jnp.max(mp_stats[:, 1], axis=0), keepdims=True)
    grad_magnitude = jnp.sqrt(squares / float(H * HD * D) + EPSILON)
    clipping = jnp.minimum(1.0, 1.0 / grad_magnitude)
    gw_ref[...] = (own_sum[...] * inverse * clipping).T.astype(BF16)
    magnitude_ref[...] = jnp.broadcast_to(grad_magnitude, magnitude_ref.shape)
    headroom_ref[...] = jnp.broadcast_to(
        jnp.log2(OVERFLOW_BOUND / (largest + EPSILON)), headroom_ref.shape
    )

    for slot in range(14):
        g_copy(me, 0, slot, across).wait_send()
    for p in range(8):
        sib_copy(p, c).wait_send()
    for direction in range(2):
        for step in range((8, 7)[direction]):
            w_copy(step, direction).wait_send()
            for half in range(2):
                r_copy(step, direction, half, part.at[half, 0]).wait_send()

    def wx_leave(i, _):
        wx_copy(i, xh).wait_send()
        return 0

    lax.fori_loop(0, NZ, wx_leave, 0)
    crossing.wait_send()
    lax.fori_loop(1, 32, leave(s_copy), 0)
    lax.fori_loop(1, 16, leave(t_copy), 0)


def shards(grad_out, queries, key_rows, value_rows, out_weight, scale_exponent):
    vmem = pl.BlockSpec(memory_space=pltpu.VMEM)
    smem = pl.BlockSpec(memory_space=pltpu.SMEM)
    dma = pltpu.SemaphoreType.DMA
    outs = pl.pallas_call(
        kernel,
        out_shape=[
            jax.ShapeDtypeStruct((TOK, HEADS), BF16),
            jax.ShapeDtypeStruct((TOK, HEADS), BF16),
            jax.ShapeDtypeStruct((TOK, HEADS), BF16),
            jax.ShapeDtypeStruct((HEADS, COLS), BF16),
            jax.ShapeDtypeStruct((8, 128), F32),
            jax.ShapeDtypeStruct((8, 128), F32),
        ],
        in_specs=[smem] + [vmem] * 5,
        out_specs=[vmem] * 6,
        scratch_shapes=[
            pltpu.VMEM((16, 2, SEQ, MINE), BF16),
            pltpu.VMEM((2, NZ, COLS, HEADS), BF16),
            pltpu.VMEM((2, NZ, COLS, HEADS), BF16),
            pltpu.VMEM((2, 8, 2, COLS, HEADS), BF16),
            pltpu.VMEM((COLS, HEADS), BF16),
            pltpu.VMEM((COLS, HEADS), BF16),
            pltpu.VMEM((4, SEQ, SEQ), F32),
            pltpu.VMEM((HEADS, TOK), BF16),
            pltpu.VMEM((TOK, HEADS), F32),
            pltpu.VMEM((TOK, HEADS), BF16),
            pltpu.VMEM((COLS, HEADS), F32),
            pltpu.VMEM((32, 2, 8, 128), F32),
            pltpu.VMEM((16, 2, 8, 128), F32),
            dma((14,)), dma((8, 2)), dma((8,)), dma((8,)),
            dma((2, 8)), dma((2, 8)), dma((NZ,)), dma((NZ,)),
            dma((2, 8, 2)), dma((2, 8, 2)), dma, dma,
            dma((32,)), dma((32,)), dma((16,)), dma((16,)),
        ],
        compiler_params=pltpu.CompilerParams(
            collective_id=0, has_side_effects=True, vmem_limit_bytes=48 * 2 ** 20
        ),
    )(scale_exponent.reshape(1), grad_out, queries, key_rows, value_rows, out_weight)
    grad_query, grad_key, grad_value, grad_weight, headroom, magnitude = outs
    return (grad_query, grad_key, grad_value, grad_weight, headroom[0, 0], magnitude[0, 0])


def solution(mesh):
    placed = (P("dp", "mp"), P("dp", "mp"), P("dp", "mp"), P("dp", "mp"), P("mp", "dp"), P())
    return jax.shard_map(
        shards,
        mesh=mesh,
        in_specs=placed,
        out_specs=(P("dp", "mp"), P("dp", "mp"), P("dp", "mp"), P("mp", "dp"), P(), P()),
        check_vma=False,
    )
```

time: 1120 us -> 124 us (0.11)
  waiting for transfers between devices: 859 us -> 0 us
  blocking collectives: 212 us -> 0 us
  Pallas kernels: 0 us -> 113 us
  between operations: 18.3 us -> 1.31 us
  matrix products: 15.8 us -> 0 us
    reduce_scatter x1 -> x0, waiting for transfers between devices: 663 us -> none  [shards(): lax.psum_scatter(partial_value.astype(jnp.float32).astype(jnp.bfloat16),...]
    all_gather x2 -> x0, waiting for transfers between devices: 195 us -> none  [the longest x1 144 us: shards(): weight_full = lax.all_gather(out_weight, 'dp', axis=1, tiled=True)]
    pallas_call x0 -> x1, Pallas kernels: none -> 113 us  [shards(): pl.pallas_call(kernel, out_shape=[jax.ShapeDtypeStruct((TOK, HEADS), BF16...]
    psum x1 -> x0, blocking collectives: 112 us -> none  [shards(): square_total = lax.psum(local_squares, ('dp', 'mp'))]
    pmax x1 -> x0, blocking collectives: 99.7 us -> none  [shards(): largest = lax.pmax(local_largest, ('dp', 'mp'))]
    dot_general x7 -> x0, matrix products: 15.3 us -> none  [the longest x1 6.97 us: shards(): jnp.einsum('th,td->hd', context, grad_full, preferred_element_type=jnp.fl...]
  transfers between devices with their start and end apart: 3 -> 0, of which waited for: 3 -> 0; matrix products, arithmetic and copies ran while one was open for 2% -> 0% of each run, Pallas kernels for 0% -> 0%
where the time goes in v1:
time: 124 us; the launch traced here: 123 us
  Pallas kernels  113 us (91%)
  local copies, waits for them, and re-layouts  8.7 us (7%)
  between operations  1.31 us (1%)
    pallas_call x1, Pallas kernels, shards(): pl.pallas_call(kernel, out_shape=[jax.ShapeDtypeStruct((TOK, HEADS), BF16...  113 us
    unnamed x13, local copies, waits for them, and re-layouts  7.68 us

profile of v1, /device:TPU:1, one launch (start us, length us, event | category | flops | bytes accessed | tf_op | source)
XLA Modules:
  0.0 123.5 jit_solution(7556489513935834153)
XLA Ops:
  1.3 1.0 copy.12.w_ref
  2.3 0.0 copy-start
  2.3 1.0 copy-done
  3.3 0.0 copy-start.1
  3.3 0.9 copy-done.1
  4.2 0.0 copy-start.2
  4.2 0.9 copy-done.2
  5.2 0.0 copy-start.3
  5.2 0.9 copy-done.3
  6.1 113.5 %shard_map.109 = (bf16[512,256]{1,0:T(8,128)(2,1)S(1)}, bf16[512,256]{1,0:T(8,128)(2,1)S(1)}, bf16[512,256]{1,0:T(8,128)(2,1)S(1)}, bf16[256,192]{1,0:T(8,128)(2...) custom-call(s32[1]{0:T(128)} %bitcast.3.exponent_ref, bf16[512,384]{1,0:T(8,128)(2,1)S(1)} %copy-done, ...), custom_call_target="tpu_custom_call" | custom-call | tf_op jit(solution)/shard_map/pallas_call | solution.py:381
  119.6 0.5 slice.7
  120.1 0.5 slice.6
  120.6 0.7 copy.13
  121.4 0.7 copy.18
  122.1 0.7 copy.19
  122.8 0.7 copy.20
Async XLA Ops:
  2.3 1.0 copy-start
  3.3 0.9 copy-start.1
  4.2 0.9 copy-start.2
  5.2 0.9 copy-start.3

commit v2 on v0

v2 whole, which is shorter than its diff:
```python
import jax
import jax.numpy as jnp
from jax import lax
from jax.experimental import pallas as pl
from jax.experimental.pallas import tpu as pltpu
from jax.sharding import PartitionSpec as P

D = 6144
H = 32
HD = 128
SEQ = 256
NZ = 16
NY = 4
TOK = 512
MINE = 384
HEADS = 256
COLS = 192

OVERFLOW_BOUND = 65504.0
EPSILON = 1e-06
MESH = pl.DeviceIdType.MESH
F32 = jnp.float32
BF16 = jnp.bfloat16


def dot(a, b, contract=((1,), (0,))):
    return lax.dot_general(a, b, (contract, ((), ())), preferred_element_type=F32)


def each(first, last, body):
    def step(i, _):
        body(i)
        return 0

    lax.fori_loop(first, last, step, 0)


def remote(source, target, send, recv, device):
    return pltpu.make_async_remote_copy(
        source, target, send, recv, device_id=device, device_id_type=MESH
    )


def kernel(
    exponent_ref, grad_hbm, q_hbm, k_hbm, v_hbm, w_hbm,
    gq_ref, gk_ref, gv_ref, gw_ref, scalars_ref,
    q_ref, k_ref, v_ref, in_sem,
    gf, wt, part, hop, xout, xin, att, ctx_t, acc, gc, own_sum, stats,
    g_send, g_recv, sib_send, sib_recv, w_send, w_recv, wx_send, wx_recv,
    r_send, r_recv, x_send, x_recv, s_send, s_recv,
):
    dp = lax.axis_index("dp")
    mp = lax.axis_index("mp")
    xh, z = dp // NZ, dp % NZ
    y, xl, c = mp // 4, (mp // 2) % 2, mp % 2
    factor = HD ** (-0.5)

    near_y = y + 1 - 2 * (y % 2)
    wide_y, opposite_y = (near_y + 2) % NY, (y + 2) % NY
    me, peer = y * 2 + xl, y * 2 + 1 - xl
    near, near_peer = near_y * 2 + xl, near_y * 2 + 1 - xl
    wide, wide_peer = wide_y * 2 + xl, wide_y * 2 + 1 - xl
    opposite, opposite_peer = opposite_y * 2 + xl, opposite_y * 2 + 1 - xl

    def to_mp(index):
        return {"dp": dp, "mp": index}

    def to_dp(index):
        return {"dp": index, "mp": mp}

    to_near, to_wide = to_mp(near * 2 + c), to_mp(wide * 2 + c)
    to_peer, to_sibling = to_mp(peer * 2 + c), to_mp(me * 2 + 1 - c)
    right, left = to_dp(xh * NZ + (z + 1) % NZ), to_dp(xh * NZ + (z + NZ - 1) % NZ)
    far = to_dp((1 - xh) * NZ + z)

    barrier = pltpu.get_barrier_semaphore()
    neighbours = (to_near, to_wide, to_peer, to_sibling, right, left, far)
    for device in neighbours:
        pl.semaphore_signal(barrier, inc=1, device_id=device, device_id_type=MESH)
    loads = [
        pltpu.make_async_copy(source, target, in_sem.at[i])
        for i, (source, target) in enumerate((
            (q_hbm, q_ref), (k_hbm, k_ref), (v_hbm, v_ref),
            (grad_hbm, gf.at[mp]), (w_hbm, wt.at[xh, z]),
        ))
    ]
    for load in loads:
        load.start()

    exponent = exponent_ref[0]
    scaling = lax.shift_left(jnp.int32(1), exponent).astype(F32)
    inverse = lax.shift_left(jnp.int32(1), 24 - exponent).astype(F32) * (2.0 ** -24)

    def g_copy(p, h, slot, device):
        piece = gf.at[p * 2 + c, h]
        return remote(piece, piece, g_send.at[slot], g_recv.at[p, h], device)

    def g_own(h, slot, device):
        return remote(
            grad_hbm.at[h], gf.at[mp, h], g_send.at[slot], g_recv.at[me, h], device
        )

    def g_wait(p, h):
        g_copy(p, h, 0, to_peer).wait_recv()

    def sib_copy(p, cc):
        piece = gf.at[p * 2 + cc]
        return remote(piece, piece, sib_send.at[p], sib_recv.at[p], to_sibling)

    def w_copy(step, direction, source=None):
        piece = wt.at[xh, (z + NZ - step) % NZ if direction == 0 else (z + step) % NZ]
        return remote(
            piece if source is None else source, piece,
            w_send.at[direction, step], w_recv.at[direction, step],
            right if direction == 0 else left,
        )

    def w_arrived(step, direction):
        index = (z + NZ - step - 1) % NZ if direction == 0 else (z + step + 1) % NZ
        piece = wt.at[xh, index]
        remote(
            piece, piece, w_send.at[direction, step], w_recv.at[direction, step],
            right if direction == 0 else left,
        ).wait_recv()

    def w_step(step):
        for direction in range(2):
            if step <= (8, 7)[direction]:
                w_arrived(step - 1, direction)
            if step < (8, 7)[direction]:
                w_copy(step, direction).start()

    def wx_copy(index, half):
        piece = wt.at[half, index]
        return remote(piece, piece, wx_send.at[index], wx_recv.at[index], far)

    def wx_start(offset):
        wx_copy((z + NZ + offset) % NZ, xh).start()

    def partial_of(m):
        block = dot(ctx_t[...], gf[m].reshape(TOK, MINE))
        turned = (block.T * scaling).astype(BF16)
        part[m // 8, 2 * (m % 8)] = turned[:COLS]
        part[m // 8, 2 * (m % 8) + 1] = turned[COLS:]

    def own_partial(p):
        partial_of(p * 2 + c)

    def sib_partial(p):
        sib_copy(p, 1 - c).wait_recv()
        partial_of(p * 2 + 1 - c)

    first = y // 2

    def half_of(turn):
        return first if turn == 0 else 1 - first

    def r_copy(step, direction, turn, source):
        return remote(
            source, hop.at[direction, step, turn],
            r_send.at[direction, step, turn], r_recv.at[direction, step, turn],
            right if direction == 0 else left,
        )

    def r_dest(step, direction):
        return (z + 8 - step) % NZ if direction == 0 else (z + NZ - 7 + step) % NZ

    def r_start(turn):
        for direction in range(2):
            r_copy(0, direction, turn, part.at[half_of(turn), r_dest(0, direction)]).start()

    def r_arrived(step, direction, turn):
        r_copy(step, direction, turn, hop.at[direction, step, turn]).wait_recv()

    def r_step(step, turn):
        for direction in range(2):
            if step < (8, 7)[direction]:
                slot = hop.at[direction, step - 1, turn]
                r_arrived(step - 1, direction, turn)
                slot[...] = (
                    slot[...].astype(F32)
                    + part[half_of(turn), r_dest(step, direction)].astype(F32)
                ).astype(BF16)
                r_copy(step, direction, turn, slot).start()

    def total(turn):
        return (
            part[half_of(turn), z].astype(F32)
            + hop[0, 7, turn].astype(F32) + hop[1, 6, turn].astype(F32)
        )

    crossing = remote(xout, xin, x_send, x_recv, far)

    def finish(turn):
        r_arrived(6, 1, turn)
        r_arrived(7, 0, turn)

        @pl.when(xh == half_of(turn))
        def _():
            own_sum[...] = total(turn)

        @pl.when(xh != half_of(turn))
        def _():
            xout[...] = total(turn).astype(BF16)
            crossing.start()

    pl.semaphore_wait(barrier, len(neighbours))
    g_own(0, 0, to_peer).start()
    g_own(0, 1, to_near).start()
    g_own(0, 2, to_wide).start()
    w_copy(0, 0, w_hbm).start()
    w_copy(0, 1, w_hbm).start()
    g_own(1, 3, to_peer).start()
    g_own(1, 4, to_near).start()
    g_own(1, 5, to_wide).start()
    remote(grad_hbm, gf.at[mp], sib_send.at[me], sib_recv.at[me], to_sibling).start()

    for load in loads:
        load.wait()
    for b in range(2):
        for h in range(2):
            rows, lanes = slice(b * SEQ, (b + 1) * SEQ), slice(h * HD, (h + 1) * HD)
            scores = dot(q_ref[rows, lanes], k_ref[rows, lanes], ((1,), (1,))) * factor
            raised = jnp.exp(scores - jnp.max(scores, axis=-1, keepdims=True))
            attention = raised / jnp.sum(raised, axis=-1, keepdims=True)
            att[b * 2 + h] = attention
            context = dot(attention.astype(BF16), v_ref[rows, lanes])
            ctx_t[lanes, rows] = context.T.astype(BF16)

    w_step(1)
    g_wait(peer, 0)
    g_copy(peer, 0, 6, to_near).start()
    own_partial(me)
    sib_partial(me)
    w_step(2)
    g_wait(near, 0)
    g_wait(near, 1)
    g_copy(near, 1, 7, to_peer).start()
    g_copy(near, 1, 8, to_wide).start()
    g_wait(peer, 1)
    g_copy(peer, 0, 9, to_wide).start()
    g_copy(peer, 1, 10, to_wide).start()
    g_wait(wide, 0)
    g_copy(wide, 0, 11, to_near).start()
    g_wait(wide, 1)
    sib_copy(peer, c).start()
    sib_copy(near, c).start()
    sib_copy(wide, c).start()
    w_step(3)
    own_partial(peer)
    own_partial(near)
    sib_partial(peer)
    sib_partial(near)
    w_step(4)
    g_wait(near_peer, 0)
    g_wait(near_peer, 1)
    sib_copy(near_peer, c).start()
    g_wait(opposite, 1)
    g_copy(opposite, 1, 12, to_peer).start()
    own_partial(near_peer)
    sib_partial(near_peer)
    r_start(0)
    w_step(5)
    own_partial(wide)
    sib_partial(wide)
    g_wait(opposite, 0)
    sib_copy(opposite, c).start()
    own_partial(opposite)
    g_wait(wide_peer, 0)
    g_copy(wide_peer, 0, 13, to_near).start()
    r_step(1, 0)
    w_step(6)
    sib_partial(opposite)
    r_step(2, 0)
    w_step(7)
    g_wait(wide_peer, 1)
    sib_copy(wide_peer, c).start()
    g_wait(opposite_peer, 1)
    g_wait(opposite_peer, 0)
    sib_copy(opposite_peer, c).start()
    own_partial(wide_peer)
    own_partial(opposite_peer)
    r_step(3, 0)
    w_step(8)
    sib_partial(wide_peer)
    sib_partial(opposite_peer)
    r_start(1)
    for offset in (0, 1, -1, 2):
        wx_start(offset)
    r_step(4, 0)
    for offset in (-2, 3, -3, 4):
        wx_start(offset)
    r_step(1, 1)
    r_step(5, 0)
    for offset in (-4, 5, -5, 6):
        wx_start(offset)
    r_step(2, 1)
    r_step(6, 0)
    for offset in (-6, 7, -7, 8):
        wx_start(offset)
    r_step(3, 1)
    r_step(7, 0)
    r_step(4, 1)
    finish(0)
    r_step(5, 1)
    for slot in range(14):
        g_copy(me, 0, slot, to_peer).wait_send()
    each(0, 8, lambda p: sib_copy(p, c).wait_send())
    r_step(6, 1)
    for direction in range(2):
        each(0, (8, 7)[direction], lambda step: w_copy(step, direction).wait_send())
    r_step(7, 1)
    finish(1)
    crossing.wait_recv()
    summed = own_sum[...] + xin[...].astype(F32)
    own_sum[...] = summed
    unscaled = summed * inverse

    def fold(a):
        return a.reshape(COLS // 8, 8, HEADS)

    squares = jnp.sum(fold(unscaled * unscaled), axis=0)
    sizes = jnp.max(fold(jnp.abs(summed)), axis=0)
    stats[0, 0, 0] = squares[:, :128] + squares[:, 128:]
    stats[0, 0, 1] = jnp.maximum(sizes[:, :128], sizes[:, 128:])

    x_core = (xh * 2 + xl) * 2 + c

    def s_targets(turn):
        if turn < 2:
            return [to_dp(xh * NZ + (z + i * 4 ** turn) % NZ) for i in range(1, 4)]
        if turn == 2:
            return [to_mp(((y + i) % NY) * 4 + xl * 2 + c) for i in range(1, 4)]
        found = []
        for i in range(1, 8):
            g = (x_core + i) % 8
            found.append({"dp": (g // 4) * NZ + z, "mp": y * 4 + g % 4})
        return found

    def s_copies(turn):
        return [
            remote(
                stats.at[turn, 0], stats.at[turn, i + 1],
                s_send.at[turn, i], s_recv.at[turn, i], device,
            )
            for i, device in enumerate(s_targets(turn))
        ]

    def s_start(turn):
        for copy in s_copies(turn):
            copy.start()

    def s_finish(turn):
        copies = s_copies(turn)
        for copy in copies:
            copy.wait_recv()
        count = len(copies) + 1
        return jnp.sum(stats[turn, :count, 0], axis=0), jnp.max(stats[turn, :count, 1], axis=0)

    s_start(0)

    each(0, NZ, lambda i: wx_copy(i, 1 - xh).wait_recv())
    acc[...] = jnp.zeros_like(acc)

    def add_context(m):
        rows = wt[m // 8, pl.ds(2 * (m % 8), 2)].reshape(MINE, HEADS)
        acc[...] += dot(gf[m].reshape(TOK, MINE), rows)

    each(0, 16, add_context)
    gc[...] = (acc[...] * scaling).astype(BF16)

    stats[1, 0, 0], stats[1, 0, 1] = s_finish(0)
    s_start(1)

    for b in range(2):
        for h in range(2):
            rows, lanes = slice(b * SEQ, (b + 1) * SEQ), slice(h * HD, (h + 1) * HD)
            attention = att[b * 2 + h]
            grad = gc[rows, lanes]
            gv_ref[rows, lanes] = (dot(attention.T.astype(BF16), grad) * inverse).astype(BF16)
            grad_attention = dot(grad, v_ref[rows, lanes], ((1,), (1,)))
            row_dots = jnp.sum(attention * grad_attention, axis=-1, keepdims=True)
            grad_scores = attention * (grad_attention - row_dots) * factor
            gq_ref[rows, lanes] = (
                dot(grad_scores.astype(BF16), k_ref[rows, lanes]) * inverse
            ).astype(BF16)
            gk_ref[rows, lanes] = (
                dot(grad_scores.T.astype(BF16), q_ref[rows, lanes]) * inverse
            ).astype(BF16)

    stats[2, 0, 0], stats[2, 0, 1] = s_finish(1)
    s_start(2)
    each(0, NZ, lambda i: wx_copy(i, xh).wait_send())
    stats[3, 0, 0], stats[3, 0, 1] = s_finish(2)
    s_start(3)
    for direction in range(2):
        for turn in range(2):
            each(
                0, (8, 7)[direction],
                lambda step: r_copy(step, direction, turn, part.at[0, 0]).wait_send(),
            )
    crossing.wait_send()
    squares, sizes = s_finish(3)
    squares, largest = jnp.sum(squares, keepdims=True), jnp.max(sizes, keepdims=True)
    grad_magnitude = jnp.sqrt(squares / float(H * HD * D) + EPSILON)
    clipping = jnp.minimum(1.0, 1.0 / grad_magnitude)
    gw_ref[...] = (own_sum[...] * inverse * clipping).astype(BF16)
    scalars_ref[0] = jnp.broadcast_to(jnp.log2(OVERFLOW_BOUND / (largest + EPSILON)), (8, 128))
    scalars_ref[1] = jnp.broadcast_to(grad_magnitude, (8, 128))
    for turn in range(4):
        for copy in s_copies(turn):
            copy.wait_send()


def hand_over(gq, gk, gv, gw, scalars, gq_out, gk_out, gv_out, gw_out, headroom, magnitude, sems):
    pairs = ((gq, gq_out), (gk, gk_out), (gv, gv_out), (gw, gw_out))
    copies = [pltpu.make_async_copy(a, b, sems.at[i]) for i, (a, b) in enumerate(pairs)]
    for copy in copies:
        copy.start()
    headroom[0] = jnp.max(scalars[0])
    magnitude[0] = jnp.max(scalars[1])
    for copy in copies:
        copy.wait()


def shards(grad_out, queries, key_rows, value_rows, out_weight, scale_exponent):
    vmem = pl.BlockSpec(memory_space=pltpu.VMEM)
    smem = pl.BlockSpec(memory_space=pltpu.SMEM)
    hbm = pl.BlockSpec(memory_space=pltpu.HBM)
    dma = pltpu.SemaphoreType.DMA
    shape = jax.ShapeDtypeStruct
    results = [shape((TOK, HEADS), BF16)] * 3 + [shape((COLS, HEADS), BF16)]
    outs = pl.pallas_call(
        kernel,
        out_shape=results + [shape((2, 8, 128), F32)],
        in_specs=[smem] + [hbm] * 5,
        out_specs=[vmem] * 5,
        scratch_shapes=[
            pltpu.VMEM((TOK, HEADS), BF16),
            pltpu.VMEM((TOK, HEADS), BF16),
            pltpu.VMEM((TOK, HEADS), BF16),
            dma((5,)),
            pltpu.VMEM((16, 2, SEQ, MINE), BF16),
            pltpu.VMEM((2, NZ, COLS, HEADS), BF16),
            pltpu.VMEM((2, NZ, COLS, HEADS), BF16),
            pltpu.VMEM((2, 8, 2, COLS, HEADS), BF16),
            pltpu.VMEM((COLS, HEADS), BF16),
            pltpu.VMEM((COLS, HEADS), BF16),
            pltpu.VMEM((4, SEQ, SEQ), F32),
            pltpu.VMEM((HEADS, TOK), BF16),
            pltpu.VMEM((TOK, HEADS), F32),
            pltpu.VMEM((TOK, HEADS), BF16),
            pltpu.VMEM((COLS, HEADS), F32),
            pltpu.VMEM((4, 8, 2, 8, 128), F32),
            dma((14,)), dma((8, 2)), dma((8,)), dma((8,)),
            dma((2, 8)), dma((2, 8)), dma((NZ,)), dma((NZ,)),
            dma((2, 8, 2)), dma((2, 8, 2)), dma, dma,
            dma((4, 7)), dma((4, 7)),
        ],
        compiler_params=pltpu.CompilerParams(
            collective_id=0, has_side_effects=True
        ),
    )(
        scale_exponent.reshape(1), grad_out.reshape(2, SEQ, MINE),
        queries, key_rows, value_rows, out_weight.T,
    )
    grad_query, grad_key, grad_value, grad_weight, headroom, magnitude = pl.pallas_call(
        hand_over,
        out_shape=results + [shape((1,), F32)] * 2,
        in_specs=[vmem] * 5,
        out_specs=[hbm] * 4 + [smem] * 2,
        scratch_shapes=[dma((4,))],
    )(*outs)
    return (
        grad_query, grad_key, grad_value, grad_weight.T,
        headroom.reshape(()), magnitude.reshape(()),
    )


def solution(mesh):
    placed = (P("dp", "mp"), P("dp", "mp"), P("dp", "mp"), P("dp", "mp"), P("mp", "dp"), P())
    return jax.shard_map(
        shards,
        mesh=mesh,
        in_specs=placed,
        out_specs=(P("dp", "mp"), P("dp", "mp"), P("dp", "mp"), P("mp", "dp"), P(), P()),
        check_vma=False,
    )
```

time: 1120 us -> 115 us (0.10)
  waiting for transfers between devices: 859 us -> 0 us
  blocking collectives: 212 us -> 0 us
  Pallas kernels: 0 us -> 114 us
  between operations: 18.3 us -> 1.29 us
  matrix products: 15.8 us -> 0 us
    reduce_scatter x1 -> x0, waiting for transfers between devices: 663 us -> none  [shards(): lax.psum_scatter(partial_value.astype(jnp.float32).astype(jnp.bfloat16),...]
    all_gather x2 -> x0, waiting for transfers between devices: 195 us -> none  [the longest x1 144 us: shards(): weight_full = lax.all_gather(out_weight, 'dp', axis=1, tiled=True)]
    pallas_call x0 -> x2, Pallas kernels: none -> 114 us  [the longest x1 111 us: shards(): pl.pallas_call(kernel, out_shape=results + [shape((2, 8, 128), F32)], in_...]
    psum x1 -> x0, blocking collectives: 112 us -> none  [shards(): square_total = lax.psum(local_squares, ('dp', 'mp'))]
    pmax x1 -> x0, blocking collectives: 99.7 us -> none  [shards(): largest = lax.pmax(local_largest, ('dp', 'mp'))]
    dot_general x7 -> x0, matrix products: 15.3 us -> none  [the longest x1 6.97 us: shards(): jnp.einsum('th,td->hd', context, grad_full, preferred_element_type=jnp.fl...]
  transfers between devices with their start and end apart: 3 -> 0, of which waited for: 3 -> 0; matrix products, arithmetic and copies ran while one was open for 2% -> 0% of each run, Pallas kernels for 0% -> 0%
where the time goes in v2:
time: 115 us
  Pallas kernels  114 us (99%)
  between operations  1.29 us (1%)
    pallas_call x1, Pallas kernels, shards(): pl.pallas_call(kernel, out_shape=results + [shape((2, 8, 128), F32)], in_...  111 us
    pallas_call x1, Pallas kernels, shards(): pl.pallas_call(hand_over, out_shape=results + [shape((1,), F32)] * 2, in_...  2.62 us

profile of v2, /device:TPU:1, one launch (start us, length us, event | category | flops | bytes accessed | tf_op | source)
XLA Modules:
  0.0 115.2 jit_solution(15530366046215223261)
XLA Ops:
  1.3 111.3 %shard_map.109 = (bf16[512,256]{1,0:T(8,128)(2,1)}, bf16[512,256]{1,0:T(8,128)(2,1)}, bf16[512,256]{1,0:T(8,128)(2,1)}, bf16[192,256]{1,0:T(8,128)(2,1)}, f32[2,8,128]{2,1,0:T(8,128)}) custom-call(s32[1]{0:T(128)} %bitcast.6.exponent_ref, bf16[2,256,384]{2,1,0:T(8,128)(2,1)} %bitcast.7, bf16[512,256]{1,0:T(8,128)(2,1)} %q_hbm.1, bf16[512,256]{1,0:T(8,128)(2,1)} %k_hbm.1, ...), custom_call_target="tpu_custom_call" | custom-call | tf_op jit(solution)/shard_map/pallas_call | solution.py:433
  112.6 2.6 %shard_map.110 = (bf16[512,256]{1,0:T(8,128)(2,1)}, bf16[512,256]{1,0:T(8,128)(2,1)}, bf16[512,256]{1,0:T(8,128)(2,1)}, bf16[192,256]{1,0:T(8,128)(2,1)}, f32[1]{0:T(128)}, /*index=5*/f32[1]{0:T(128)}) custom-call(bf16[512,256]{1,0:T(8,128)(2,1)} %get-tuple-element.17.gq, bf16[512,256]{1,0:T(8,128)(2,1)} %get-tuple-element.18.gk, ...), custom_call_target="tpu_custom_call" | custom-call | tf_op jit(solution)/shard_map/pallas_call | solution.py:467

commit v3 on v2

--- a/solution.py
+++ b/solution.py
@@ -15,6 +15,7 @@
 MINE = 384
 HEADS = 256
 COLS = 192
+CUT = COLS // 2
 
 OVERFLOW_BOUND = 65504.0
 EPSILON = 1e-06
@@ -134,8 +135,35 @@
         piece = wt.at[half, index]
         return remote(piece, piece, wx_send.at[index], wx_recv.at[index], far)
 
-    def wx_start(offset):
-        wx_copy((z + NZ + offset) % NZ, xh).start()
+    def pair_of(order):
+        return (z // 2 + (0, 1, 7, 2, 6, 3, 5, 4)[order]) % 8
+
+    def wx_pair(order):
+        for i in range(2):
+            wx_copy(2 * pair_of(order) + i, xh).start()
+
+    def add_context(order):
+        pair = pair_of(order)
+        for i in range(2):
+            wx_copy(2 * pair + i, 1 - xh).wait_recv()
+        for half in range(2):
+            rows = wt[half, pl.ds(2 * pair, 2)].reshape(MINE, HEADS)
+            acc[...] += dot(gf[half * 8 + pair].reshape(TOK, MINE), rows)
+
+    def attention_backward(b, h):
+        rows, lanes = slice(b * SEQ, (b + 1) * SEQ), slice(h * HD, (h + 1) * HD)
+        attention = att[b * 2 + h]
+        grad = gc[rows, lanes]
+        gv_ref[rows, lanes] = (dot(attention.T.astype(BF16), grad) * inverse).astype(BF16)
+        grad_attention = dot(grad, v_ref[rows, lanes], ((1,), (1,)))
+        row_dots = jnp.sum(attention * grad_attention, axis=-1, keepdims=True)
+        grad_scores = attention * (grad_attention - row_dots) * factor
+        gq_ref[rows, lanes] = (
+            dot(grad_scores.astype(BF16), k_ref[rows, lanes]) * inverse
+        ).astype(BF16)
+        gk_ref[rows, lanes] = (
+            dot(grad_scores.T.astype(BF16), q_ref[rows, lanes]) * inverse
+        ).astype(BF16)
 
     def partial_of(m):
         block = dot(ctx_t[...], gf[m].reshape(TOK, MINE))
@@ -155,45 +183,49 @@
     def half_of(turn):
         return first if turn == 0 else 1 - first
 
-    def r_copy(step, direction, turn, source):
+    def r_copy(step, direction, turn, piece, source):
         return remote(
-            source, hop.at[direction, step, turn],
-            r_send.at[direction, step, turn], r_recv.at[direction, step, turn],
+            source, hop.at[direction, step, turn, piece],
+            r_send.at[direction, step, turn, piece], r_recv.at[direction, step, turn, piece],
             right if direction == 0 else left,
         )
 
-    def r_dest(step, direction):
-        return (z + 8 - step) % NZ if direction == 0 else (z + NZ - 7 + step) % NZ
+    def r_part(step, direction, turn, piece):
+        dest = (z + 8 - step) % NZ if direction == 0 else (z + NZ - 7 + step) % NZ
+        return part.at[half_of(turn), dest, piece * CUT : (piece + 1) * CUT]
 
     def r_start(turn):
-        for direction in range(2):
-            r_copy(0, direction, turn, part.at[half_of(turn), r_dest(0, direction)]).start()
-
-    def r_arrived(step, direction, turn):
-        r_copy(step, direction, turn, hop.at[direction, step, turn]).wait_recv()
+        for piece in range(2):
+            for direction in range(2):
+                r_copy(0, direction, turn, piece, r_part(0, direction, turn, piece)).start()
+
+    def r_arrived(step, direction, turn, piece):
+        r_copy(step, direction, turn, piece, hop.at[direction, step, turn, piece]).wait_recv()
 
     def r_step(step, turn):
-        for direction in range(2):
-            if step < (8, 7)[direction]:
-                slot = hop.at[direction, step - 1, turn]
-                r_arrived(step - 1, direction, turn)
-                slot[...] = (
-                    slot[...].astype(F32)
-                    + part[half_of(turn), r_dest(step, direction)].astype(F32)
-                ).astype(BF16)
-                r_copy(step, direction, turn, slot).start()
+        for piece in range(2):
+            for direction in range(2):
+                if step < (8, 7)[direction]:
+                    slot = hop.at[direction, step - 1, turn, piece]
+                    r_arrived(step - 1, direction, turn, piece)
+                    slot[...] = (
+                        slot[...].astype(F32) + r_part(step, direction, turn, piece)[...].astype(F32)
+                    ).astype(BF16)
+                    r_copy(step, direction, turn, piece, slot).start()
 
     def total(turn):
         return (
             part[half_of(turn), z].astype(F32)
-            + hop[0, 7, turn].astype(F32) + hop[1, 6, turn].astype(F32)
+            + hop[0, 7, turn].reshape(COLS, HEADS).astype(F32)
+            + hop[1, 6, turn].reshape(COLS, HEADS).astype(F32)
         )
 
     crossing = remote(xout, xin, x_send, x_recv, far)
 
     def finish(turn):
-        r_arrived(6, 1, turn)
-        r_arrived(7, 0, turn)
+        for piece in range(2):
+            r_arrived(6, 1, turn, piece)
+            r_arrived(7, 0, turn, piece)
 
         @pl.when(xh == half_of(turn))
         def _():
@@ -205,14 +237,20 @@
             crossing.start()
 
     pl.semaphore_wait(barrier, len(neighbours))
-    g_own(0, 0, to_peer).start()
-    g_own(0, 1, to_near).start()
-    g_own(0, 2, to_wide).start()
+    own_to_peer = [g_own(0, 0, to_peer), g_own(1, 3, to_peer)]
+    own_to_near = [g_own(0, 1, to_near), g_own(1, 4, to_near)]
+    own_to_wide = [g_own(0, 2, to_wide), g_own(1, 5, to_wide)]
+    peer_to_near, near_to_peer = g_copy(peer, 0, 6, to_near), g_copy(near, 1, 7, to_peer)
+    near_to_wide = g_copy(near, 1, 8, to_wide)
+    peer_to_wide = [g_copy(peer, 0, 9, to_wide), g_copy(peer, 1, 10, to_wide)]
+    wide_to_near, opposite_to_peer = g_copy(wide, 0, 11, to_near), g_copy(opposite, 1, 12, to_peer)
+    wide_peer_to_near = g_copy(wide_peer, 0, 13, to_near)
+
+    own_to_near[0].start()
+    own_to_peer[0].start()
+    own_to_wide[0].start()
     w_copy(0, 0, w_hbm).start()
     w_copy(0, 1, w_hbm).start()
-    g_own(1, 3, to_peer).start()
-    g_own(1, 4, to_near).start()
-    g_own(1, 5, to_wide).start()
     remote(grad_hbm, gf.at[mp], sib_send.at[me], sib_recv.at[me], to_sibling).start()
 
     for load in loads:
@@ -227,90 +265,113 @@
             context = dot(attention.astype(BF16), v_ref[rows, lanes])
             ctx_t[lanes, rows] = context.T.astype(BF16)
 
+    for sends in (own_to_near, own_to_peer, own_to_wide):
+        sends[0].wait_send()
+        sends[1].start()
     w_step(1)
-    g_wait(peer, 0)
-    g_copy(peer, 0, 6, to_near).start()
     own_partial(me)
     sib_partial(me)
     w_step(2)
+    g_wait(peer, 0)
+    own_to_near[1].wait_send()
+    peer_to_near.start()
+    g_wait(near, 1)
+    own_to_peer[1].wait_send()
+    near_to_peer.start()
+    own_to_wide[1].wait_send()
+    near_to_wide.start()
+    g_wait(peer, 1)
+    sib_copy(peer, c).start()
     g_wait(near, 0)
-    g_wait(near, 1)
-    g_copy(near, 1, 7, to_peer).start()
-    g_copy(near, 1, 8, to_wide).start()
-    g_wait(peer, 1)
-    g_copy(peer, 0, 9, to_wide).start()
-    g_copy(peer, 1, 10, to_wide).start()
-    g_wait(wide, 0)
-    g_copy(wide, 0, 11, to_near).start()
-    g_wait(wide, 1)
-    sib_copy(peer, c).start()
     sib_copy(near, c).start()
-    sib_copy(wide, c).start()
-    w_step(3)
     own_partial(peer)
     own_partial(near)
+    g_wait(wide, 0)
+    g_wait(wide, 1)
+    sib_copy(wide, c).start()
     sib_partial(peer)
     sib_partial(near)
-    w_step(4)
+    w_step(3)
+    peer_to_near.wait_send()
+    wide_to_near.start()
+    near_to_wide.wait_send()
+    peer_to_wide[0].start()
     g_wait(near_peer, 0)
     g_wait(near_peer, 1)
     sib_copy(near_peer, c).start()
     g_wait(opposite, 1)
-    g_copy(opposite, 1, 12, to_peer).start()
+    near_to_peer.wait_send()
+    opposite_to_peer.start()
     own_partial(near_peer)
     sib_partial(near_peer)
     r_start(0)
-    w_step(5)
+    w_step(4)
     own_partial(wide)
     sib_partial(wide)
+    wide_to_near.wait_send()
+    g_wait(wide_peer, 0)
+    wide_peer_to_near.start()
+    peer_to_wide[0].wait_send()
+    peer_to_wide[1].start()
     g_wait(opposite, 0)
     sib_copy(opposite, c).start()
+    wx_pair(0)
+    r_step(1, 0)
     own_partial(opposite)
-    g_wait(wide_peer, 0)
-    g_copy(wide_peer, 0, 13, to_near).start()
-    r_step(1, 0)
-    w_step(6)
+    w_step(5)
     sib_partial(opposite)
-    r_step(2, 0)
-    w_step(7)
     g_wait(wide_peer, 1)
     sib_copy(wide_peer, c).start()
     g_wait(opposite_peer, 1)
     g_wait(opposite_peer, 0)
     sib_copy(opposite_peer, c).start()
+    r_step(2, 0)
     own_partial(wide_peer)
     own_partial(opposite_peer)
-    r_step(3, 0)
-    w_step(8)
     sib_partial(wide_peer)
     sib_partial(opposite_peer)
     r_start(1)
-    for offset in (0, 1, -1, 2):
-        wx_start(offset)
+    wx_pair(1)
+    w_step(6)
+    r_step(3, 0)
+    r_step(1, 1)
+    wx_pair(2)
+    w_step(7)
     r_step(4, 0)
-    for offset in (-2, 3, -3, 4):
-        wx_start(offset)
-    r_step(1, 1)
+    r_step(2, 1)
+    w_step(8)
+    wx_pair(3)
+    wx_pair(4)
+    acc[...] = jnp.zeros_like(acc)
     r_step(5, 0)
-    for offset in (-4, 5, -5, 6):
-        wx_start(offset)
-    r_step(2, 1)
+    r_step(3, 1)
+    wx_pair(5)
+    wx_pair(6)
+    add_context(0)
     r_step(6, 0)
-    for offset in (-6, 7, -7, 8):
-        wx_start(offset)
-    r_step(3, 1)
+    r_step(4, 1)
+    wx_pair(7)
+    add_context(1)
     r_step(7, 0)
-    r_step(4, 1)
+    r_step(5, 1)
+    add_context(2)
+    add_context(3)
     finish(0)
-    r_step(5, 1)
-    for slot in range(14):
-        g_copy(me, 0, slot, to_peer).wait_send()
+    r_step(6, 1)
+    for copy in (peer_to_wide[1], opposite_to_peer, wide_peer_to_near):
+        copy.wait_send()
     each(0, 8, lambda p: sib_copy(p, c).wait_send())
-    r_step(6, 1)
+    add_context(4)
+    add_context(5)
+    r_step(7, 1)
     for direction in range(2):
         each(0, (8, 7)[direction], lambda step: w_copy(step, direction).wait_send())
-    r_step(7, 1)
+    add_context(6)
     finish(1)
+    add_context(7)
+    gc[...] = (acc[...] * scaling).astype(BF16)
+    attention_backward(0, 0)
+    attention_backward(0, 1)
     crossing.wait_recv()
     summed = own_sum[...] + xin[...].astype(F32)
     own_sum[...] = summed
@@ -359,45 +420,23 @@
 
     s_start(0)
 
-    each(0, NZ, lambda i: wx_copy(i, 1 - xh).wait_recv())
-    acc[...] = jnp.zeros_like(acc)
-
-    def add_context(m):
-        rows = wt[m // 8, pl.ds(2 * (m % 8), 2)].reshape(MINE, HEADS)
-        acc[...] += dot(gf[m].reshape(TOK, MINE), rows)
-
-    each(0, 16, add_context)
-    gc[...] = (acc[...] * scaling).astype(BF16)
-
+    attention_backward(1, 0)
     stats[1, 0, 0], stats[1, 0, 1] = s_finish(0)
     s_start(1)
-
-    for b in range(2):
-        for h in range(2):
-            rows, lanes = slice(b * SEQ, (b + 1) * SEQ), slice(h * HD, (h + 1) * HD)
-            attention = att[b * 2 + h]
-            grad = gc[rows, lanes]
-            gv_ref[rows, lanes] = (dot(attention.T.astype(BF16), grad) * inverse).astype(BF16)
-            grad_attention = dot(grad, v_ref[rows, lanes], ((1,), (1,)))
-            row_dots = jnp.sum(attention * grad_attention, axis=-1, keepdims=True)
-            grad_scores = attention * (grad_attention - row_dots) * factor
-            gq_ref[rows, lanes] = (
-                dot(grad_scores.astype(BF16), k_ref[rows, lanes]) * inverse
-            ).astype(BF16)
-            gk_ref[rows, lanes] = (
-                dot(grad_scores.T.astype(BF16), q_ref[rows, lanes]) * inverse
-            ).astype(BF16)
-
+    each(0, NZ, lambda i: wx_copy(i, xh).wait_send())
+    attention_backward(1, 1)
     stats[2, 0, 0], stats[2, 0, 1] = s_finish(1)
     s_start(2)
-    each(0, NZ, lambda i: wx_copy(i, xh).wait_send())
     stats[3, 0, 0], stats[3, 0, 1] = s_finish(2)
     s_start(3)
     for direction in range(2):
         for turn in range(2):
             each(
                 0, (8, 7)[direction],
-                lambda step: r_copy(step, direction, turn, part.at[0, 0]).wait_send(),
+                lambda step: [
+                    r_copy(step, direction, turn, piece, part.at[0, 0, :CUT]).wait_send()
+                    for piece in range(2)
+                ],
             )
     crossing.wait_send()
     squares, sizes = s_finish(3)
@@ -443,7 +482,7 @@
             pltpu.VMEM((16, 2, SEQ, MINE), BF16),
             pltpu.VMEM((2, NZ, COLS, HEADS), BF16),
             pltpu.VMEM((2, NZ, COLS, HEADS), BF16),
-            pltpu.VMEM((2, 8, 2, COLS, HEADS), BF16),
+            pltpu.VMEM((2, 8, 2, 2, CUT, HEADS), BF16),
             pltpu.VMEM((COLS, HEADS), BF16),
             pltpu.VMEM((COLS, HEADS), BF16),
             pltpu.VMEM((4, SEQ, SEQ), F32),
@@ -454,7 +493,7 @@
             pltpu.VMEM((4, 8, 2, 8, 128), F32),
             dma((14,)), dma((8, 2)), dma((8,)), dma((8,)),
             dma((2, 8)), dma((2, 8)), dma((NZ,)), dma((NZ,)),
-            dma((2, 8, 2)), dma((2, 8, 2)), dma, dma,
+            dma((2, 8, 2, 2)), dma((2, 8, 2, 2)), dma, dma,
             dma((4, 7)), dma((4, 7)),
         ],
         compiler_params=pltpu.CompilerParams(

time: 115 us -> 106 us (0.922)
  Pallas kernels: 114 us -> 105 us
    pallas_call x1, Pallas kernels: 111 us -> 102 us  [shards(): pl.pallas_call(kernel, out_shape=results + [shape((2, 8, 128), F32)], in_...]
where the time goes in v3:
time: 106 us
  Pallas kernels  105 us (99%)
  between operations  1.29 us (1%)
    pallas_call x1, Pallas kernels, shards(): pl.pallas_call(kernel, out_shape=results + [shape((2, 8, 128), F32)], in_...  102 us
    pallas_call x1, Pallas kernels, shards(): pl.pallas_call(hand_over, out_shape=results + [shape((1,), F32)] * 2, in_...  2.62 us

profile of v3, /device:TPU:1, one launch (start us, length us, event | category | flops | bytes accessed | tf_op | source)
XLA Modules:
  0.0 106.3 jit_solution(12686785525947251488)
XLA Ops:
  1.3 102.3 %shard_map.109 = (bf16[512,256]{1,0:T(8,128)(2,1)}, bf16[512,256]{1,0:T(8,128)(2,1)}, bf16[512,256]{1,0:T(8,128)(2,1)}, bf16[192,256]{1,0:T(8,128)(2,1)}, f32[2,8,128]{2,1,0:T(8,128)}) custom-call(s32[1]{0:T(128)} %bitcast.6.exponent_ref, bf16[2,256,384]{2,1,0:T(8,128)(2,1)} %bitcast.7, bf16[512,256]{1,0:T(8,128)(2,1)} %q_hbm.1, bf16[512,256]{1,0:T(8,128)(2,1)} %k_hbm.1, ...), custom_call_target="tpu_custom_call" | custom-call | tf_op jit(solution)/shard_map/pallas_call | solution.py:472
  103.6 2.6 %shard_map.110 = (bf16[512,256]{1,0:T(8,128)(2,1)}, bf16[512,256]{1,0:T(8,128)(2,1)}, bf16[512,256]{1,0:T(8,128)(2,1)}, bf16[192,256]{1,0:T(8,128)(2,1)}, f32[1]{0:T(128)}, /*index=5*/f32[1]{0:T(128)}) custom-call(bf16[512,256]{1,0:T(8,128)(2,1)} %get-tuple-element.17.gq, bf16[512,256]{1,0:T(8,128)(2,1)} %get-tuple-element.18.gk, ...), custom_call_target="tpu_custom_call" | custom-call | tf_op jit(solution)/shard_map/pallas_call | solution.py:506

commit v4 on v3

--- a/solution.py
+++ b/solution.py
@@ -36,6 +36,14 @@
     lax.fori_loop(first, last, step, 0)
 
 
+def wrap(a, n):
+    return lax.rem(a, jnp.int32(n))
+
+
+def over(a, n):
+    return lax.div(a, jnp.int32(n))
+
+
 def remote(source, target, send, recv, device):
     return pltpu.make_async_remote_copy(
         source, target, send, recv, device_id=device, device_id_type=MESH
@@ -44,20 +52,20 @@
 
 def kernel(
     exponent_ref, grad_hbm, q_hbm, k_hbm, v_hbm, w_hbm,
-    gq_ref, gk_ref, gv_ref, gw_ref, scalars_ref,
-    q_ref, k_ref, v_ref, in_sem,
+    gq_hbm, gk_hbm, gv_hbm, gw_ref, scalars_ref,
+    q_ref, k_ref, v_ref, in_sem, gq_ref, gk_ref, gv_ref, out_sem,
     gf, wt, part, hop, xout, xin, att, ctx_t, acc, gc, own_sum, stats,
     g_send, g_recv, sib_send, sib_recv, w_send, w_recv, wx_send, wx_recv,
     r_send, r_recv, x_send, x_recv, s_send, s_recv,
 ):
     dp = lax.axis_index("dp")
     mp = lax.axis_index("mp")
-    xh, z = dp // NZ, dp % NZ
-    y, xl, c = mp // 4, (mp // 2) % 2, mp % 2
+    xh, z = over(dp, NZ), wrap(dp, NZ)
+    y, xl, c = over(mp, 4), wrap(over(mp, 2), 2), wrap(mp, 2)
     factor = HD ** (-0.5)
 
-    near_y = y + 1 - 2 * (y % 2)
-    wide_y, opposite_y = (near_y + 2) % NY, (y + 2) % NY
+    near_y = y + 1 - 2 * wrap(y, 2)
+    wide_y, opposite_y = wrap(near_y + 2, NY), wrap(y + 2, NY)
     me, peer = y * 2 + xl, y * 2 + 1 - xl
     near, near_peer = near_y * 2 + xl, near_y * 2 + 1 - xl
     wide, wide_peer = wide_y * 2 + xl, wide_y * 2 + 1 - xl
@@ -71,7 +79,8 @@
 
     to_near, to_wide = to_mp(near * 2 + c), to_mp(wide * 2 + c)
     to_peer, to_sibling = to_mp(peer * 2 + c), to_mp(me * 2 + 1 - c)
-    right, left = to_dp(xh * NZ + (z + 1) % NZ), to_dp(xh * NZ + (z + NZ - 1) % NZ)
+    right = to_dp(xh * NZ + wrap(z + 1, NZ))
+    left = to_dp(xh * NZ + wrap(z + NZ - 1, NZ))
     far = to_dp((1 - xh) * NZ + z)
 
     barrier = pltpu.get_barrier_semaphore()
@@ -109,7 +118,7 @@
         return remote(piece, piece, sib_send.at[p], sib_recv.at[p], to_sibling)
 
     def w_copy(step, direction, source=None):
-        piece = wt.at[xh, (z + NZ - step) % NZ if direction == 0 else (z + step) % NZ]
+        piece = wt.at[xh, wrap(z + NZ - step if direction == 0 else z + step, NZ)]
         return remote(
             piece if source is None else source, piece,
             w_send.at[direction, step], w_recv.at[direction, step],
@@ -117,7 +126,7 @@
         )
 
     def w_arrived(step, direction):
-        index = (z + NZ - step - 1) % NZ if direction == 0 else (z + step + 1) % NZ
+        index = wrap(z + NZ - step - 1 if direction == 0 else z + step + 1, NZ)
         piece = wt.at[xh, index]
         remote(
             piece, piece, w_send.at[direction, step], w_recv.at[direction, step],
@@ -136,7 +145,7 @@
         return remote(piece, piece, wx_send.at[index], wx_recv.at[index], far)
 
     def pair_of(order):
-        return (z // 2 + (0, 1, 7, 2, 6, 3, 5, 4)[order]) % 8
+        return wrap(over(z, 2) + (0, 1, 7, 2, 6, 3, 5, 4)[order], 8)
 
     def wx_pair(order):
         for i in range(2):
@@ -168,8 +177,9 @@
     def partial_of(m):
         block = dot(ctx_t[...], gf[m].reshape(TOK, MINE))
         turned = (block.T * scaling).astype(BF16)
-        part[m // 8, 2 * (m % 8)] = turned[:COLS]
-        part[m // 8, 2 * (m % 8) + 1] = turned[COLS:]
+        half, pair = over(m, 8), wrap(m, 8)
+        part[half, 2 * pair] = turned[:COLS]
+        part[half, 2 * pair + 1] = turned[COLS:]
 
     def own_partial(p):
         partial_of(p * 2 + c)
@@ -178,7 +188,7 @@
         sib_copy(p, 1 - c).wait_recv()
         partial_of(p * 2 + 1 - c)
 
-    first = y // 2
+    first = over(y, 2)
 
     def half_of(turn):
         return first if turn == 0 else 1 - first
@@ -191,7 +201,7 @@
         )
 
     def r_part(step, direction, turn, piece):
-        dest = (z + 8 - step) % NZ if direction == 0 else (z + NZ - 7 + step) % NZ
+        dest = wrap(z + 8 - step if direction == 0 else z + NZ - 7 + step, NZ)
         return part.at[half_of(turn), dest, piece * CUT : (piece + 1) * CUT]
 
     def r_start(turn):
@@ -213,28 +223,28 @@
                     ).astype(BF16)
                     r_copy(step, direction, turn, piece, slot).start()
 
-    def total(turn):
+    def total(turn, piece):
         return (
-            part[half_of(turn), z].astype(F32)
-            + hop[0, 7, turn].reshape(COLS, HEADS).astype(F32)
-            + hop[1, 6, turn].reshape(COLS, HEADS).astype(F32)
+            r_part(8, 0, turn, piece)[...].astype(F32)
+            + hop[0, 7, turn, piece].astype(F32) + hop[1, 6, turn, piece].astype(F32)
         )
 
-    crossing = remote(xout, xin, x_send, x_recv, far)
+    def crossing(piece):
+        return remote(xout.at[piece], xin.at[piece], x_send.at[piece], x_recv.at[piece], far)
 
     def finish(turn):
         for piece in range(2):
+            r_arrived(7, 0, turn, piece)
             r_arrived(6, 1, turn, piece)
-            r_arrived(7, 0, turn, piece)
-
-        @pl.when(xh == half_of(turn))
-        def _():
-            own_sum[...] = total(turn)
-
-        @pl.when(xh != half_of(turn))
-        def _():
-            xout[...] = total(turn).astype(BF16)
-            crossing.start()
+
+            @pl.when(xh == half_of(turn))
+            def _():
+                own_sum[piece] = total(turn, piece)
+
+            @pl.when(xh != half_of(turn))
+            def _():
+                xout[piece] = total(turn, piece).astype(BF16)
+                crossing(piece).start()
 
     pl.semaphore_wait(barrier, len(neighbours))
     own_to_peer = [g_own(0, 0, to_peer), g_own(1, 3, to_peer)]
@@ -372,9 +382,10 @@
     gc[...] = (acc[...] * scaling).astype(BF16)
     attention_backward(0, 0)
     attention_backward(0, 1)
-    crossing.wait_recv()
-    summed = own_sum[...] + xin[...].astype(F32)
-    own_sum[...] = summed
+    for piece in range(2):
+        crossing(piece).wait_recv()
+        own_sum[piece] += xin[piece].astype(F32)
+    summed = own_sum[...].reshape(COLS, HEADS)
     unscaled = summed * inverse
 
     def fold(a):
@@ -389,13 +400,13 @@
 
     def s_targets(turn):
         if turn < 2:
-            return [to_dp(xh * NZ + (z + i * 4 ** turn) % NZ) for i in range(1, 4)]
+            return [to_dp(xh * NZ + wrap(z + i * 4 ** turn, NZ)) for i in (2, 3, 1)]
         if turn == 2:
-            return [to_mp(((y + i) % NY) * 4 + xl * 2 + c) for i in range(1, 4)]
+            return [to_mp(wrap(y + i, NY) * 4 + xl * 2 + c) for i in (2, 1, 3)]
         found = []
-        for i in range(1, 8):
-            g = (x_core + i) % 8
-            found.append({"dp": (g // 4) * NZ + z, "mp": y * 4 + g % 4})
+        for i in (4, 5, 3, 2, 6, 1, 7):
+            g = wrap(x_core + i, 8)
+            found.append({"dp": over(g, 4) * NZ + z, "mp": y * 4 + wrap(g, 4)})
         return found
 
     def s_copies(turn):
@@ -425,6 +436,14 @@
     s_start(1)
     each(0, NZ, lambda i: wx_copy(i, xh).wait_send())
     attention_backward(1, 1)
+    stores = [
+        pltpu.make_async_copy(source, target, out_sem.at[i])
+        for i, (source, target) in enumerate(
+            ((gq_ref, gq_hbm), (gk_ref, gk_hbm), (gv_ref, gv_hbm))
+        )
+    ]
+    for store in stores:
+        store.start()
     stats[2, 0, 0], stats[2, 0, 1] = s_finish(1)
     s_start(2)
     stats[3, 0, 0], stats[3, 0, 1] = s_finish(2)
@@ -438,17 +457,22 @@
                     for piece in range(2)
                 ],
             )
-    crossing.wait_send()
+    for piece in range(2):
+        crossing(piece).wait_send()
+    for store in stores:
+        store.wait()
+    for turn in range(3):
+        for copy in s_copies(turn):
+            copy.wait_send()
     squares, sizes = s_finish(3)
     squares, largest = jnp.sum(squares, keepdims=True), jnp.max(sizes, keepdims=True)
     grad_magnitude = jnp.sqrt(squares / float(H * HD * D) + EPSILON)
     clipping = jnp.minimum(1.0, 1.0 / grad_magnitude)
-    gw_ref[...] = (own_sum[...] * inverse * clipping).astype(BF16)
+    gw_ref[...] = (own_sum[...].reshape(COLS, HEADS) * inverse * clipping).astype(BF16)
     scalars_ref[0] = jnp.broadcast_to(jnp.log2(OVERFLOW_BOUND / (largest + EPSILON)), (8, 128))
     scalars_ref[1] = jnp.broadcast_to(grad_magnitude, (8, 128))
-    for turn in range(4):
-        for copy in s_copies(turn):
-            copy.wait_send()
+    for copy in s_copies(3):
+        copy.wait_send()
 
 
 def hand_over(gq, gk, gv, gw, scalars, gq_out, gk_out, gv_out, gw_out, headroom, magnitude, sems):
@@ -473,27 +497,31 @@
         kernel,
         out_shape=results + [shape((2, 8, 128), F32)],
         in_specs=[smem] + [hbm] * 5,
-        out_specs=[vmem] * 5,
+        out_specs=[hbm] * 3 + [vmem] * 2,
         scratch_shapes=[
             pltpu.VMEM((TOK, HEADS), BF16),
             pltpu.VMEM((TOK, HEADS), BF16),
             pltpu.VMEM((TOK, HEADS), BF16),
             dma((5,)),
+            pltpu.VMEM((TOK, HEADS), BF16),
+            pltpu.VMEM((TOK, HEADS), BF16),
+            pltpu.VMEM((TOK, HEADS), BF16),
+            dma((3,)),
             pltpu.VMEM((16, 2, SEQ, MINE), BF16),
             pltpu.VMEM((2, NZ, COLS, HEADS), BF16),
             pltpu.VMEM((2, NZ, COLS, HEADS), BF16),
             pltpu.VMEM((2, 8, 2, 2, CUT, HEADS), BF16),
-            pltpu.VMEM((COLS, HEADS), BF16),
-            pltpu.VMEM((COLS, HEADS), BF16),
+            pltpu.VMEM((2, CUT, HEADS), BF16),
+            pltpu.VMEM((2, CUT, HEADS), BF16),
             pltpu.VMEM((4, SEQ, SEQ), F32),
             pltpu.VMEM((HEADS, TOK), BF16),
             pltpu.VMEM((TOK, HEADS), F32),
             pltpu.VMEM((TOK, HEADS), BF16),
-            pltpu.VMEM((COLS, HEADS), F32),
+            pltpu.VMEM((2, CUT, HEADS), F32),
             pltpu.VMEM((4, 8, 2, 8, 128), F32),
             dma((14,)), dma((8, 2)), dma((8,)), dma((8,)),
             dma((2, 8)), dma((2, 8)), dma((NZ,)), dma((NZ,)),
-            dma((2, 8, 2, 2)), dma((2, 8, 2, 2)), dma, dma,
+            dma((2, 8, 2, 2)), dma((2, 8, 2, 2)), dma((2,)), dma((2,)),
             dma((4, 7)), dma((4, 7)),
         ],
         compiler_params=pltpu.CompilerParams(

time: 106 us -> 105 us (level)
    pallas_call x1, Pallas kernels: 102 us -> 101 us  [shards(): pl.pallas_call(kernel, out_shape=results + [shape((2, 8, 128), F32)], in_...]
where the time goes in v4:
time: 105 us
  Pallas kernels  104 us (99%)
  between operations  1.29 us (1%)
    pallas_call x1, Pallas kernels, shards(): pl.pallas_call(kernel, out_shape=results + [shape((2, 8, 128), F32)], in_...  101 us
    pallas_call x1, Pallas kernels, shards(): pl.pallas_call(hand_over, out_shape=results + [shape((1,), F32)] * 2, in_...  2.62 us

profile of v4, /device:TPU:1, one launch (start us, length us, event | category | flops | bytes accessed | tf_op | source)
XLA Modules:
  0.0 105.2 jit_solution(13707359531216674524)
XLA Ops:
  1.3 101.3 %shard_map.109 = (bf16[512,256]{1,0:T(8,128)(2,1)}, bf16[512,256]{1,0:T(8,128)(2,1)}, bf16[512,256]{1,0:T(8,128)(2,1)}, bf16[192,256]{1,0:T(8,128)(2,1)}, f32[2,8,128]{2,1,0:T(8,128)}) custom-call(s32[1]{0:T(128)} %bitcast.6.exponent_ref, bf16[2,256,384]{2,1,0:T(8,128)(2,1)} %bitcast.7, bf16[512,256]{1,0:T(8,128)(2,1)} %q_hbm.1, bf16[512,256]{1,0:T(8,128)(2,1)} %k_hbm.1, ...), custom_call_target="tpu_custom_call" | custom-call | tf_op jit(solution)/shard_map/pallas_call | solution.py:496
  102.6 2.6 %shard_map.110 = (bf16[512,256]{1,0:T(8,128)(2,1)}, bf16[512,256]{1,0:T(8,128)(2,1)}, bf16[512,256]{1,0:T(8,128)(2,1)}, bf16[192,256]{1,0:T(8,128)(2,1)}, f32[1]{0:T(128)}, /*index=5*/f32[1]{0:T(128)}) custom-call(bf16[512,256]{1,0:T(8,128)(2,1)} %get-tuple-element.17.gq, bf16[512,256]{1,0:T(8,128)(2,1)} %get-tuple-element.18.gk, ...), custom_call_target="tpu_custom_call" | custom-call | tf_op jit(solution)/shard_map/pallas_call | solution.py:534

commit v5 on v4

--- a/solution.py
+++ b/solution.py
@@ -475,15 +475,28 @@
         copy.wait_send()
 
 
-def hand_over(gq, gk, gv, gw, scalars, gq_out, gk_out, gv_out, gw_out, headroom, magnitude, sems):
-    pairs = ((gq, gq_out), (gk, gk_out), (gv, gv_out), (gw, gw_out))
-    copies = [pltpu.make_async_copy(a, b, sems.at[i]) for i, (a, b) in enumerate(pairs)]
-    for copy in copies:
-        copy.start()
+def hand_over(
+    gq, gk, gv, gw, scalars, gq_out, gk_out, gv_out, gw_out, headroom, magnitude,
+    gq_held, gk_held, gv_held, gw_held, in_sem, out_sem,
+):
+    held = (gq_held, gk_held, gv_held, gw_held)
+    loads = [
+        pltpu.make_async_copy(source, block, in_sem.at[i])
+        for i, (source, block) in enumerate(zip((gq, gk, gv, gw), held))
+    ]
+    stores = [
+        pltpu.make_async_copy(block, target, out_sem.at[i])
+        for i, (block, target) in enumerate(zip(held, (gq_out, gk_out, gv_out, gw_out)))
+    ]
+    for load in loads:
+        load.start()
     headroom[0] = jnp.max(scalars[0])
     magnitude[0] = jnp.max(scalars[1])
-    for copy in copies:
-        copy.wait()
+    for load, store in zip(loads, stores):
+        load.wait()
+        store.start()
+    for store in stores:
+        store.wait()
 
 
 def shards(grad_out, queries, key_rows, value_rows, out_weight, scale_exponent):
@@ -534,9 +547,10 @@
     grad_query, grad_key, grad_value, grad_weight, headroom, magnitude = pl.pallas_call(
         hand_over,
         out_shape=results + [shape((1,), F32)] * 2,
-        in_specs=[vmem] * 5,
+        in_specs=[hbm] * 4 + [vmem],
         out_specs=[hbm] * 4 + [smem] * 2,
-        scratch_shapes=[dma((4,))],
+        scratch_shapes=[pltpu.VMEM((TOK, HEADS), BF16)] * 3
+        + [pltpu.VMEM((COLS, HEADS), BF16), dma((4,)), dma((4,))],
     )(*outs)
     return (
         grad_query, grad_key, grad_value, grad_weight.T,

time: 105 us -> 106 us (level)
  no operation moved by 1% of the time
where the time goes in v5:
time: 106 us
  Pallas kernels  104 us (98%)
  between operations  1.29 us (1%)
    pallas_call x1, Pallas kernels, shards(): pl.pallas_call(kernel, out_shape=results + [shape((2, 8, 128), F32)], in_...  101 us
    pallas_call x1, Pallas kernels, shards(): pl.pallas_call(hand_over, out_shape=results + [shape((1,), F32)] * 2, in_...  3.14 us

profile of v5, /device:TPU:1, one launch (start us, length us, event | category | flops | bytes accessed | tf_op | source)
XLA Modules:
  0.0 105.7 jit_solution(3644143770910174980)
XLA Ops:
  1.3 101.3 %shard_map.109 = (bf16[512,256]{1,0:T(8,128)(2,1)}, bf16[512,256]{1,0:T(8,128)(2,1)}, bf16[512,256]{1,0:T(8,128)(2,1)}, bf16[192,256]{1,0:T(8,128)(2,1)}, f32[2,8,128]{2,1,0:T(8,128)}) custom-call(s32[1]{0:T(128)} %bitcast.6.exponent_ref, bf16[2,256,384]{2,1,0:T(8,128)(2,1)} %bitcast.7, bf16[512,256]{1,0:T(8,128)(2,1)} %q_hbm.1, bf16[512,256]{1,0:T(8,128)(2,1)} %k_hbm.1, ...), custom_call_target="tpu_custom_call" | custom-call | tf_op jit(solution)/shard_map/pallas_call | solution.py:509
  102.6 3.1 %shard_map.110 = (bf16[512,256]{1,0:T(8,128)(2,1)}, bf16[512,256]{1,0:T(8,128)(2,1)}, bf16[512,256]{1,0:T(8,128)(2,1)}, bf16[192,256]{1,0:T(8,128)(2,1)}, f32[1]{0:T(128)}, /*index=5*/f32[1]{0:T(128)}) custom-call(bf16[512,256]{1,0:T(8,128)(2,1)} %get-tuple-element.17.gq, bf16[512,256]{1,0:T(8,128)(2,1)} %get-tuple-element.18.gk, ...), custom_call_target="tpu_custom_call" | custom-call | tf_op jit(solution)/shard_map/pallas_call | solution.py:547
